TPU v7x, 32 devices: a whole 2x2x4 slice. The times are simulated.
32 devices in a mesh: dp: 16 (over z, y, x), tensor: 2 (over core).
Axes of the slice: x: 2, y: 2, z: 4, core: 2. Of those that a mesh axis runs over, the one named last changes fastest.
Arguments:
- inputs: bfloat16 [32768, 512], P(('dp', 'tensor')), may hold values from -6 to 6
- lengths: int32 [128], P('dp'), may hold values from 1 to 250, 12288 in all
- w_query: bfloat16 [512, 512], P(None, 'tensor'), may hold values from -0.25 to 0.25
- w_key: bfloat16 [512, 512], P(None, 'tensor'), may hold values from -0.25 to 0.25
- w_value: bfloat16 [512, 512], P(None, 'tensor'), may hold values from -0.25 to 0.25
- w_attn_out: bfloat16 [512, 512], P('tensor'), may hold values from -1.25 to 1.25
- gain_attn: float32 [512], replicated, may hold values from 0.5 to 1.5
- offset_attn: float32 [512], replicated, may hold values from -2 to 2
- w_in: bfloat16 [512, 2048], P(None, 'tensor'), may hold values from -0.25 to 0.25
- b_in: bfloat16 [2048], P('tensor'), may hold values from -3 to 3
- w_out: bfloat16 [2048, 512], P('tensor'), may hold values from -0.125 to 0.125
- b_out: float32 [512], replicated, may hold values from -2 to 2
- gain_ffn: float32 [512], replicated, may hold values from 0.5 to 1.5
- offset_ffn: float32 [512], replicated, may hold values from -2 to 2
- cotangent: bfloat16 [32768, 512], P(('dp', 'tensor')), may hold values from -6 to 6
Outputs:
- output: bfloat16 [32768, 512], P(('dp', 'tensor'))
- grad_inputs: float32 [32768, 512], P(('dp', 'tensor'))
- grad_query: float32 [512, 512], P(None, 'tensor')
- grad_key: float32 [512, 512], P(None, 'tensor')
- grad_value: float32 [512, 512], P(None, 'tensor')
- grad_attn_out: float32 [512, 512], P('tensor')
- grad_gain_attn: float32 [512], replicated
- grad_offset_attn: float32 [512], replicated
- grad_w_in: float32 [512, 2048], P(None, 'tensor')
- grad_b_in: float32 [2048], P('tensor')
- grad_w_out: float32 [2048, 512], P('tensor')
- grad_b_out: float32 [512], replicated
- grad_gain_ffn: float32 [512], replicated
- grad_offset_ffn: float32 [512], replicated
Inputs may be any that keep to these rules, and one draw needn't show every extreme that they name: Batch row b holds one sentence of lengths[b] subwords at its first positions; the rest of its 256 positions are padding.
All inputs are finite; a program needn't handle non-finite values. No bound on the sum of `lengths` on one device may be relied on, other than what follows from the above.
Results may differ from a plain program's by a relative error of at most 0.039.
Values may be sent and summed in bfloat16 or wider, within the bound.
A program may use at most 192 MiB of HBM per device.

v0:
```python
import jax
import jax.numpy as jnp
from jax import lax
from jax.sharding import PartitionSpec as P

HEAD_DIM = 64
SEQ = 256
RECUR = 2


epsilon = 1e-05
masked_score = -1e30


def layer_norm(resid, gain_vec, offset):
    row_mean = jnp.mean(resid, axis=-1, keepdims=True)
    centred = resid - row_mean
    spread = jnp.mean(centred * centred, axis=-1, keepdims=True)
    return centred * lax.rsqrt(spread + epsilon) * gain_vec + offset


def block_scores(queries, key_block, sent_lens):
    scores = jnp.einsum("bqhd,bkhd->bhqk", queries, key_block, preferred_element_type=jnp.float32)
    scores = scores * HEAD_DIM ** (-0.5)
    places = lax.broadcasted_iota(jnp.int32, (sent_lens.shape[0], SEQ), 1)
    usable = places < sent_lens[:, None]
    return jnp.where(usable[:, None, None, :], scores, masked_score)


def attend_block(record):
    queries, key_block, values, sent_lens = record
    scores = block_scores(queries, key_block, sent_lens)
    maximum = jnp.max(scores, axis=-1, keepdims=True)
    exponent = jnp.exp(scores - maximum)
    row_total = jnp.sum(exponent, axis=-1, keepdims=True)
    probability = (exponent / row_total).astype(jnp.bfloat16)
    context = jnp.einsum("bhqk,bkhd->bqhd", probability, values, preferred_element_type=jnp.float32)
    return (context.astype(jnp.bfloat16), maximum[..., 0] + jnp.log(row_total[..., 0]))


def attend_back(record):
    queries, key_block, values, sent_lens, logsum, grad_context = record
    scores = block_scores(queries, key_block, sent_lens)
    attn_weights = jnp.exp(scores - logsum[..., None])
    probability = attn_weights.astype(jnp.bfloat16)
    grad_values = jnp.einsum(
        "bhqk,bqhd->bkhd", probability, grad_context, preferred_element_type=jnp.float32
    )
    grad_prob = jnp.einsum(
        "bqhd,bkhd->bhqk", grad_context, values, preferred_element_type=jnp.float32
    )
    inner_sum = jnp.sum(grad_prob * attn_weights, axis=-1, keepdims=True)
    grad_scores = (attn_weights * (grad_prob - inner_sum)).astype(jnp.bfloat16)
    score_scale = HEAD_DIM ** (-0.5)
    grad_queries = (
        jnp.einsum("bhqk,bkhd->bqhd", grad_scores, key_block, preferred_element_type=jnp.float32)
        * score_scale
    )
    grad_keys = (
        jnp.einsum("bhqk,bqhd->bkhd", grad_scores, queries, preferred_element_type=jnp.float32)
        * score_scale
    )
    return (
        grad_queries.astype(jnp.bfloat16),
        grad_keys.astype(jnp.bfloat16),
        grad_values.astype(jnp.bfloat16),
    )


def to_blocks(matrix, row_count, pair_size):
    head_count = matrix.shape[1] // HEAD_DIM
    return matrix.reshape(row_count // pair_size, pair_size, SEQ, head_count, HEAD_DIM)


def split_packed(packed, row_count, pair_size):
    head_cols = packed.shape[1] // 3
    return tuple(
        (
            to_blocks(
                packed[:, column * head_cols : (column + 1) * head_cols], row_count, pair_size
            )
            for column in range(3)
        )
    )


def attention(packed, sent_lens):
    row_count = sent_lens.shape[0]
    pair_size = 2
    head_cols = packed.shape[1] // 3
    pieces = split_packed(packed, row_count, pair_size)
    context, logsum = lax.map(
        attend_block, pieces + (sent_lens.reshape(row_count // pair_size, pair_size),)
    )
    return (context.reshape(row_count * SEQ, head_cols), logsum)


def attention_back(packed, sent_lens, logsum, grad_context):
    row_count = sent_lens.shape[0]
    pair_size = 2
    head_cols = packed.shape[1] // 3
    pieces = split_packed(packed, row_count, pair_size)
    records = pieces + (
        sent_lens.reshape(row_count // pair_size, pair_size),
        logsum,
        to_blocks(grad_context, row_count, pair_size),
    )
    grads = lax.map(attend_back, records)
    return jnp.concatenate([grad.reshape(row_count * SEQ, head_cols) for grad in grads], axis=1)


def layer_forward(stream, sent_lens, params):
    w_packed, w_attn_out, gain_attn, offset_attn, w_in, b_in, w_out, b_out, gain_ffn, offset_ffn = (
        params
    )
    rows_full = lax.all_gather(stream.astype(jnp.bfloat16), "tensor", axis=0, tiled=True)
    packed = jnp.dot(rows_full, w_packed, preferred_element_type=jnp.float32).astype(jnp.bfloat16)
    context, logsum = attention(packed, sent_lens)
    attn_share = lax.psum_scatter(
        jnp.dot(context, w_attn_out, preferred_element_type=jnp.float32).astype(jnp.bfloat16),
        "tensor",
        scatter_dimension=0,
        tiled=True,
    ).astype(jnp.float32)
    middle = layer_norm(stream + attn_share, gain_attn, offset_attn)
    middle_full = lax.all_gather(middle.astype(jnp.bfloat16), "tensor", axis=0, tiled=True)
    hidden = jnp.dot(middle_full, w_in, preferred_element_type=jnp.float32) + b_in.astype(
        jnp.float32
    )
    active = jax.nn.gelu(hidden).astype(jnp.bfloat16)
    ffn_share = lax.psum_scatter(
        jnp.dot(active, w_out, preferred_element_type=jnp.float32).astype(jnp.bfloat16),
        "tensor",
        scatter_dimension=0,
        tiled=True,
    ).astype(jnp.float32)
    ffn_share = ffn_share + b_out
    result = layer_norm(middle + ffn_share, gain_ffn, offset_ffn)
    kept = (
        stream,
        rows_full,
        packed,
        context,
        logsum,
        attn_share,
        middle,
        middle_full,
        hidden,
        active,
        ffn_share,
    )
    return (result, kept)


def layer_backward(grad_result, kept, sent_lens, params):
    w_packed, w_attn_out, gain_attn, offset_attn, w_in, b_in, w_out, b_out, gain_ffn, offset_ffn = (
        params
    )
    (
        stream,
        rows_full,
        packed,
        context,
        logsum,
        attn_share,
        middle,
        middle_full,
        hidden,
        active,
        ffn_share,
    ) = kept
    _, norm_back = jax.vjp(layer_norm, middle + ffn_share, gain_ffn, offset_ffn)
    grad_sum_ffn, grad_gain_ffn, grad_offset_ffn = norm_back(grad_result)
    grad_branch = grad_sum_ffn.astype(jnp.bfloat16)
    grad_b_out = jnp.sum(grad_branch.astype(jnp.float32), axis=0)
    branch_full = lax.all_gather(grad_branch, "tensor", axis=0, tiled=True)
    grad_w_out = jnp.einsum("tf,td->fd", active, branch_full, preferred_element_type=jnp.float32)
    grad_active = jnp.einsum("td,fd->tf", branch_full, w_out, preferred_element_type=jnp.float32)
    _, gelu_back = jax.vjp(jax.nn.gelu, hidden)
    grad_hidden = gelu_back(grad_active)[0].astype(jnp.bfloat16)
    grad_b_in = jnp.sum(grad_hidden.astype(jnp.float32), axis=0)
    grad_w_in = jnp.einsum(
        "td,tf->df", middle_full, grad_hidden, preferred_element_type=jnp.float32
    )
    grad_middle = grad_sum_ffn + lax.psum_scatter(
        jnp.einsum("tf,df->td", grad_hidden, w_in, preferred_element_type=jnp.float32).astype(
            jnp.bfloat16
        ),
        "tensor",
        scatter_dimension=0,
        tiled=True,
    ).astype(jnp.float32)
    _, norm_back_attn = jax.vjp(layer_norm, stream + attn_share, gain_attn, offset_attn)
    grad_sum_attn, grad_gain_attn, grad_offset_attn = norm_back_attn(grad_middle)
    grad_attn = grad_sum_attn.astype(jnp.bfloat16)
    attn_full = lax.all_gather(grad_attn, "tensor", axis=0, tiled=True)
    grad_w_attn_out = jnp.einsum(
        "tc,td->cd", context, attn_full, preferred_element_type=jnp.float32
    )
    grad_context = jnp.einsum(
        "td,cd->tc", attn_full, w_attn_out, preferred_element_type=jnp.float32
    ).astype(jnp.bfloat16)
    grad_packed = attention_back(packed, sent_lens, logsum, grad_context)
    grad_w_packed = jnp.einsum(
        "td,tc->dc", rows_full, grad_packed, preferred_element_type=jnp.float32
    )
    grad_stream = grad_sum_attn + lax.psum_scatter(
        jnp.einsum("tc,dc->td", grad_packed, w_packed, preferred_element_type=jnp.float32).astype(
            jnp.bfloat16
        ),
        "tensor",
        scatter_dimension=0,
        tiled=True,
    ).astype(jnp.float32)
    head_cols = w_packed.shape[1] // 3
    wide = (
        grad_w_packed[:, :head_cols],
        grad_w_packed[:, head_cols : 2 * head_cols],
        grad_w_packed[:, 2 * head_cols :],
        grad_w_in,
        grad_w_attn_out,
        grad_w_out,
        grad_b_in,
    )
    small = (grad_gain_attn, grad_offset_attn, grad_b_out, grad_gain_ffn, grad_offset_ffn)
    return (grad_stream, wide, small)


def reduce_grads(wide, small):
    wide = lax.psum(wide, "dp")
    small = lax.psum(small, ("dp", "tensor"))
    return (wide, small)


def shards(
    inputs,
    lengths,
    w_query,
    w_key,
    w_value,
    w_attn_out,
    gain_attn,
    offset_attn,
    w_in,
    b_in,
    w_out,
    b_out,
    gain_ffn,
    offset_ffn,
    cotangent,
):
    w_packed = jnp.concatenate([w_query, w_key, w_value], axis=1)
    full_attn_out, full_in, full_out, full_b_in = (w_attn_out, w_in, w_out, b_in)
    params = (
        w_packed,
        full_attn_out,
        gain_attn,
        offset_attn,
        full_in,
        full_b_in,
        full_out,
        b_out,
        gain_ffn,
        offset_ffn,
    )
    stream = inputs.astype(jnp.float32)
    stored = []
    for recurrence in range(RECUR):
        stream_in = stream
        stream, kept = layer_forward(stream_in, lengths, params)
        stored.append(stream_in)
    output = stream.astype(jnp.bfloat16)
    grad_stream = cotangent.astype(jnp.float32)
    wide_total = ()
    small_total = ()
    for recurrence in reversed(range(RECUR)):
        kept = layer_forward(stored[recurrence], lengths, params)[1]
        grad_stream, wide, small = layer_backward(grad_stream, kept, lengths, params)
        if recurrence == RECUR - 1:
            wide_total, small_total = (wide, small)
        else:
            wide_total = jax.tree.map(jnp.add, wide_total, wide)
            small_total = jax.tree.map(jnp.add, small_total, small)
    wide_total, small_total = reduce_grads(wide_total, small_total)
    return (
        output,
        grad_stream,
        wide_total[0],
        wide_total[1],
        wide_total[2],
        wide_total[4],
        small_total[0],
        small_total[1],
        wide_total[3],
        wide_total[6],
        wide_total[5],
        small_total[2],
        small_total[3],
        small_total[4],
    )


def solution(mesh):
    in_specs = (
        P(("dp", "tensor"), None),
        P("dp"),
        P(None, "tensor"),
        P(None, "tensor"),
        P(None, "tensor"),
        P("tensor", None),
        P(),
        P(),
        P(None, "tensor"),
        P("tensor"),
        P("tensor", None),
        P(),
        P(),
        P(),
        P(("dp", "tensor"), None),
    )
    out_specs = (
        P(("dp", "tensor"), None),
        P(("dp", "tensor"), None),
        P(None, "tensor"),
        P(None, "tensor"),
        P(None, "tensor"),
        P("tensor", None),
        P(),
        P(),
        P(None, "tensor"),
        P("tensor"),
        P("tensor", None),
        P(),
        P(),
        P(),
    )
    return jax.shard_map(shards, mesh=mesh, in_specs=in_specs, out_specs=out_specs, check_vma=False)
```

profile of v0, /device:TPU:0, one launch (start us, length us, event | category | flops | bytes accessed | tf_op | source)
XLA Modules:
  0.0 843.1 jit_solution(9187966603925743623)
XLA Ops:
  10.7 12.2 %all-gather.11.cloned.1.call-done = bf16[2048,512]{1,0:T(8,128)(2,1)} async-done(((bf16[1024,512]{1,0:T(8,128)(2,1)}), bf16[2048,512]{1,0:T(8,128)(2,1)}) %all-gather.11.cloned.1.call-update) | async-done | bytes 2097168 | tf_op jit(solution)/shard_map/all_gather | solution.py:116
  22.9 3.4 fusion.188
  38.2 17.6 %while.76 = (s32[]{:T(128)}, bf16[4,2,256,4,64]{2,1,0,4,3:T(2,128)(2,1)}, f32[4,2,4,256]{3,2,1,0:T(4,128)}, bf16[4,2,256,4,64]{2,4,3,1,0:T(8,128)(2,1)}, s32[4,2...) while((s32[]{:T(128)}, ...), condition=%wide.region_42.43_spmd, body=%wide.region_39.42_spmd.sunk | while | flops 140638720 | bytes 7935089 | solution.py:92
  61.4 22.6 %while.72 = (s32[]{:T(128)}, bf16[4,2,256,4,64]{2,1,0,4,3:T(2,128)(2,1)S(1)}, bf16[4,2,256,4,64]{2,4,3,1,0:T(8,128)(2,1)}, s32[4,2]{1,0:T(4,128)S(1)}, bf16[4,2,...) while((s32[]{:T(128)}, bf16[4,2,256,4,64]{2,1,0,4,3:T(2,128)(2,1)S(1)}, ...), condition=%wide.region_3.4_spmd, body=%wide.region_0.3_spmd.sunk | while | flops 137495296 | bytes 5786733 | solution.py:92
  89.5 10.6 %reduce-scatter.13.cloned.1.call-done = bf16[1024,512]{1,0:T(8,128)(2,1)} async-done(((bf16[2048,512]{1,0:T(8,128)(2,1)}), bf16[1024,512]{1,0:T(8,128)(2,1)}) %reduce-scatter.13.cloned.1.call-update) | async-done | bytes 1048592 | tf_op jit(solution)/shard_map/reduce_scatter | solution.py:119
  106.6 11.3 %all-gather.25.cloned.1.call-done = bf16[2048,512]{1,0:T(8,128)(2,1)} async-done(((bf16[1024,512]{1,0:T(8,128)(2,1)}), bf16[2048,512]{1,0:T(8,128)(2,1)}) %all-gather.25.cloned.1.call-update) | async-done | bytes 2097168 | tf_op jit(solution)/shard_map/all_gather | solution.py:126
  117.8 4.1 fusion.243
  125.2 4.3 convolution_convert_fusion.9
  131.6 7.5 fusion.182
  139.2 5.9 reduce-scatter.31.cloned.1.call-done
  145.1 13.8 %reduce-scatter.15.cloned.1.call-done = bf16[1024,512]{1,0:T(8,128)(2,1)} async-done(((bf16[2048,512]{1,0:T(8,128)(2,1)}), bf16[1024,512]{1,0:T(8,128)(2,1)}) %reduce-scatter.15.cloned.1.call-update) | async-done | bytes 1048592 | tf_op jit(solution)/shard_map/reduce_scatter | solution.py:131
  158.8 4.6 fusion.227
  166.6 11.5 %all-gather.15.cloned.1.call-done = bf16[2048,512]{1,0:T(8,128)(2,1)} async-done(((bf16[1024,512]{1,0:T(8,128)(2,1)}), bf16[2048,512]{1,0:T(8,128)(2,1)}) %all-gather.15.cloned.1.call-update) | async-done | bytes 2097168 | tf_op jit(solution)/shard_map/all_gather | solution.py:116
  178.0 3.4 convolution_convert_fusion.6
  188.6 4.4 reshape.458
  202.0 20.9 %while.73 = (s32[]{:T(128)}, bf16[4,2,256,4,64]{2,1,0,4,3:T(2,128)(2,1)}, bf16[4,2,256,4,64]{2,4,3,1,0:T(8,128)(2,1)}, s32[4,2]{1,0:T(4,128)S(1)}, bf16[4,2,256,...) while((s32[]{:T(128)}, bf16[4,2,256,4,64]{2,1,0,4,3:T(2,128)(2,1)}, ...), condition=%wide.region_13.14_spmd, body=%wide.region_10.13_spmd.sunk | while | flops 137495296 | bytes 5787241 | solution.py:92
  230.7 15.4 %while.74 = (s32[]{:T(128)}, bf16[4,2,256,4,64]{2,1,0,4,3:T(2,128)(2,1)}, f32[4,2,4,256]{3,2,1,0:T(4,128)S(1)}, bf16[4,2,256,4,64]{2,4,3,1,0:T(8,128)(2,1)}, s32...) while((s32[]{:T(128)}, ...), condition=%wide.region_23.24_spmd, body=%wide.region_20.23_spmd.sunk | while | flops 140638720 | bytes 7934581 | solution.py:92
  252.6 10.9 %reduce-scatter.21.cloned.1.call-done = bf16[1024,512]{1,0:T(8,128)(2,1)} async-done(((bf16[2048,512]{1,0:T(8,128)(2,1)}), bf16[1024,512]{1,0:T(8,128)(2,1)}) %reduce-scatter.21.cloned.1.call-update) | async-done | bytes 1048592 | tf_op jit(solution)/shard_map/reduce_scatter | solution.py:119
  270.3 11.3 %all-gather.19.cloned.1.call-done = bf16[2048,512]{1,0:T(8,128)(2,1)} async-done(((bf16[1024,512]{1,0:T(8,128)(2,1)}), bf16[2048,512]{1,0:T(8,128)(2,1)}) %all-gather.19.cloned.1.call-update) | async-done | bytes 2097168 | tf_op jit(solution)/shard_map/all_gather | solution.py:126
  281.6 8.1 multiply_convert_fusion.3
  291.7 3.7 convolution_convert_fusion.12
  295.7 7.6 fusion.185
  303.3 5.7 reduce-scatter.23.cloned.1.call-done
  309.0 13.6 %reduce-scatter.19.cloned.1.call-done = bf16[1024,512]{1,0:T(8,128)(2,1)} async-done(((bf16[2048,512]{1,0:T(8,128)(2,1)}), bf16[1024,512]{1,0:T(8,128)(2,1)}) %reduce-scatter.19.cloned.1.call-update) | async-done | bytes 1048592 | tf_op jit(solution)/shard_map/reduce_scatter | solution.py:131
  322.6 4.1 fusion.225
  333.6 11.9 %all-gather.21.cloned.1.call-done = bf16[2048,512]{1,0:T(8,128)(2,1)} async-done(((bf16[1024,512]{1,0:T(8,128)(2,1)}), bf16[2048,512]{1,0:T(8,128)(2,1)}) %all-gather.21.cloned.1.call-update) | async-done | bytes 2097168 | tf_op jit(solution)/shard_map/all_gather | solution.py:176
  345.4 11.0 %convert_reduce_fusion.1 = (f32[1024]{0:T(1024)}, bf16[2048,1024]{1,0:T(8,128)(2,1)S(1)}) fusion(f32[2048,1024]{1,0:T(8,128)} %get-tuple-element.546, f32[1024]{0:T(1024)S(1)} %convert_element_type.254, bf16[2048,512]{1,0:T(8,128)(2,1)} %all-gather.21.cloned.1.call-done, bf16[1024,512]{1,0:T(8,128)(2,1)} %param.37), kind=kOutput, calls=%fused_computation.213 | convolution fusion | flops 2195717120 | bytes 15736832 | tf_op jit(solution)/shard_map/td,fd->tf/dot_general | solution.py:178
  358.4 3.8 convolution_convert_fusion.11
  362.6 10.5 %reduce-scatter.25.cloned.1.call-done = bf16[1024,512]{1,0:T(8,128)(2,1)} async-done(((bf16[2048,512]{1,0:T(8,128)(2,1)}), bf16[1024,512]{1,0:T(8,128)(2,1)}) %reduce-scatter.25.cloned.1.call-update) | async-done | bytes 1048592 | tf_op jit(solution)/shard_map/reduce_scatter | solution.py:185
  373.1 3.4 multiply_reduce_fusion.4
  380.5 11.9 %all-gather.23.cloned.1.call-done = bf16[2048,512]{1,0:T(8,128)(2,1)} async-done(((bf16[1024,512]{1,0:T(8,128)(2,1)}), bf16[2048,512]{1,0:T(8,128)(2,1)}) %all-gather.23.cloned.1.call-update) | async-done | bytes 2097168 | tf_op jit(solution)/shard_map/all_gather | solution.py:196
  405.7 26.4 %while.75 = (s32[]{:T(128)}, bf16[4,2,256,4,64]{2,1,0,4,3:T(2,128)(2,1)}, bf16[4,2,256,4,64]{2,1,0,4,3:T(2,128)(2,1)}, bf16[4,2,256,4,64]{2,1,0,4,3:T(2,128)(2,1...) while((s32[]{:T(128)}, ...), condition=%wide.region_37.38_spmd, body=%wide.region_35.37_spmd.sunk | while | flops 340916736 | bytes 24162996 | solution.py:108
  443.1 5.1 convolution_convert_fusion.17
  450.9 8.2 reduce-scatter.27.cloned.1.call-done
  467.5 11.9 %all-gather.27.cloned.1.call-done = bf16[2048,512]{1,0:T(8,128)(2,1)} async-done(((bf16[1024,512]{1,0:T(8,128)(2,1)}), bf16[2048,512]{1,0:T(8,128)(2,1)}) %all-gather.27.cloned.1.call-update) | async-done | bytes 2097168 | tf_op jit(solution)/shard_map/all_gather | solution.py:176
  479.4 10.7 %convert_reduce_fusion = (f32[1024]{0:T(1024)S(1)}, bf16[2048,1024]{1,0:T(8,128)(2,1)S(1)}) fusion(f32[2048,1024]{1,0:T(8,128)} %copy-done.91, f32[1024]{0:T(1024)S(1)} %convert_element_type.254, bf16[2048,512]{1,0:T(8,128)(2,1)} %all-gather.27.cloned.1.call-done, bf16[1024,512]{1,0:T(8,128)(2,1)S(1)} %copy-done.90), kind=kOutput, calls=%fused_computation.212 | convolution fusion | flops 2195717120 | bytes 15736832 | tf_op jit(solution)/shard_map/td,fd->tf/dot_general | solution.py:178
  492.0 3.8 convolution_convert_fusion.8
  495.9 10.9 %reduce-scatter.33.cloned.1.call-done = bf16[1024,512]{1,0:T(8,128)(2,1)} async-done(((bf16[2048,512]{1,0:T(8,128)(2,1)}), bf16[1024,512]{1,0:T(8,128)(2,1)}) %reduce-scatter.33.cloned.1.call-update) | async-done | bytes 1048592 | tf_op jit(solution)/shard_map/reduce_scatter | solution.py:185
  514.4 5.9 fusion.247
  520.3 5.3 all-gather.29.cloned.1.call-done
  539.0 27.9 %while.77 = (s32[]{:T(128)}, bf16[4,2,256,4,64]{2,1,0,4,3:T(2,128)(2,1)}, bf16[4,2,256,4,64]{2,1,0,4,3:T(2,128)(2,1)}, bf16[4,2,256,4,64]{2,1,0,4,3:T(2,128)(2,1...) while((s32[]{:T(128)}, ...), condition=%wide.region_56.57_spmd, body=%wide.region_54.56_spmd.sunk | while | flops 340916736 | bytes 24162996 | solution.py:108
  577.9 5.1 convolution_convert_fusion.16
  583.3 5.3 fusion.246
  594.0 3.8 convolution_add_fusion.1
  598.7 5.1 convolution_add_fusion
  610.5 44.6 %psum.91 = f32[1024]{0:T(1024)} all-reduce(f32[1024]{0:T(1024)S(1)} %add.415), channel_id=1, replica_groups=mesh['dp'=16,'tensor'=2] {'dp'}, use_global_device_ids=true, to_apply=%region_71.72 | all-reduce | flops 1024 | bytes 8192 | tf_op jit(solution)/shard_map/psum | solution.py:230
  655.1 37.7 %all-reduce = (f32[512]{0:T(512)}, f32[512]{0:T(512)}, f32[512]{0:T(512)}, f32[512]{0:T(512)}, f32[512]{0:T(512)}) all-reduce(f32[512]{0:T(512)S(1)} %add.412, f32[512]{0:T(512)S(1)} %add.413, f32[512]{0:T(512)S(1)} %add.417, f32[512]{0:T(512)S(1)} %add.418, f32[512]{0:T(512)S(1)} %add.419), channel_id=1, replica_groups=mesh['dp'=16,'tensor'=2] {'dp','tensor'}, use_global_device_ids=true, to_apply=%region_64.65 | all-reduce | flops 2560 | bytes 20480 | tf_op jit(solution)/shard_map/psum | solution.py:231
  695.6 131.4 %all-reduce.4.cloned.1.call-done = (f32[512,256]{1,0:T(8,128)}, f32[512,256]{1,0:T(8,128)}, f32[512,256]{1,0:T(8,128)}, f32[256,512]{1,0:T(8,128)}, f32[512,1024]{1,0:T(8,128)}, /*index=5*/f32[1024,512]{1,0:T(8,128)}) async-done(((f32[512,256]{1,0:T(8,128)}, f32[512,256]{1,0:T(8,128)}, f32[512,256]{1,0:T(8,128)}, f32[256,512]{1,0:T(8,128)}, f32[512,1024]{1,0:T(8,128)}, /*index=5*/f32[1024,512]{1,0:T(8,128)}), ...) | async-done | bytes 6291472 | tf_op jit(solution)/shard_map/psum | solution.py:230
  (558 shorter events, 318.4 us)
Async XLA Ops:
  7.2 110.7 %copy-start = (bf16[512,1024]{1,0:T(8,128)(2,1)S(1)}, bf16[512,1024]{1,0:T(8,128)(2,1)}, u32[]{:S(2)}) copy-start(bf16[512,1024]{1,0:T(8,128)(2,1)} %param.35) | copy-start | bytes 3145732
  7.2 15.7 %all-gather.11.cloned.1.call-start = ((), (), s32[]{:S(2)}) async-start(), calls=%async_computation.12 | async-start | bytes 3145728 | tf_op jit(solution)/shard_map/all_gather | solution.py:116
  7.9 81.6 %reduce-scatter.29.cloned.1.call-start = ((), (), s32[]{:S(2)}) async-start(), calls=%async_computation.27 | async-start | bytes 3145728 | tf_op jit(solution)/shard_map/reduce_scatter | solution.py:119
  10.7 15.6 %copy-start.67 = (bf16[512,768]{1,0:T(8,128)(2,1)}, bf16[512,768]{1,0:T(8,128)(2,1)S(1)}, u32[]{:S(2)}) copy-start(bf16[512,768]{1,0:T(8,128)(2,1)S(1)} %constant_dynamic-update-slice_fusion) | copy-start | bytes 2359300
  60.8 39.3 %reduce-scatter.13.cloned.1.call-start = ((), (), s32[]{:S(2)}) async-start(), calls=%async_computation.13 | async-start | bytes 3145728 | tf_op jit(solution)/shard_map/reduce_scatter | solution.py:119
  89.2 10.9 %copy-start.1 = (bf16[1024,512]{1,0:T(8,128)(2,1)S(1)}, bf16[1024,512]{1,0:T(8,128)(2,1)}, u32[]{:S(2)}) copy-start(bf16[1024,512]{1,0:T(8,128)(2,1)} %param.27) | copy-start | bytes 3145732
  89.2 28.6 %all-gather.25.cloned.1.call-start = ((), (), s32[]{:S(2)}) async-start(), calls=%async_computation.28 | async-start | bytes 3145728 | tf_op jit(solution)/shard_map/all_gather | solution.py:126
  89.5 13.0 %copy-start.3 = (bf16[1024,512]{1,0:T(8,128)(2,1)S(1)}, bf16[1024,512]{1,0:T(8,128)(2,1)}, u32[]{:S(2)}) copy-start(bf16[1024,512]{1,0:T(8,128)(2,1)} %reduce-scatter.29.cloned.1.call-done) | copy-start | bytes 3145732
  102.5 56.3 %copy-start.62 = (f32[1024]{0:T(1024)}, f32[1024]{0:T(1024)S(1)}, u32[]{:S(2)}) copy-start(f32[1024]{0:T(1024)S(1)} %get-tuple-element.551) | copy-start | bytes 12292
  103.7 55.1 %copy-start.65 = (f32[1024]{0:T(1024)}, f32[1024]{0:T(1024)S(1)}, u32[]{:S(2)}) copy-start(f32[1024]{0:T(1024)S(1)} %fusion.208) | copy-start | bytes 12292
  105.9 25.7 %all-gather.13.cloned.1.call-start = ((), (), s32[]{:S(2)}) async-start(), calls=%async_computation.14 | async-start | bytes 3145728 | tf_op jit(solution)/shard_map/all_gather | solution.py:126
  106.5 38.5 %reduce-scatter.31.cloned.1.call-start = ((), (), s32[]{:S(2)}) async-start(), calls=%async_computation.29 | async-start | bytes 3145728 | tf_op jit(solution)/shard_map/reduce_scatter | solution.py:131
  117.8 7.4 copy-start.88
  129.6 29.2 %reduce-scatter.15.cloned.1.call-start = ((), (), s32[]{:S(2)}) async-start(), calls=%async_computation.15 | async-start | bytes 3145728 | tf_op jit(solution)/shard_map/reduce_scatter | solution.py:131
  139.1 19.7 %copy-start.82 = (f32[512]{0:T(512)S(1)}, f32[512]{0:T(512)}, u32[]{:S(2)}) copy-start(f32[512]{0:T(512)} %param.38) | copy-start | bytes 6148
  139.1 38.9 %all-gather.15.cloned.1.call-start = ((), (), s32[]{:S(2)}) async-start(), calls=%async_computation.16 | async-start | bytes 3145728 | tf_op jit(solution)/shard_map/all_gather | solution.py:116
  164.7 13.3 %copy-start.68 = (bf16[512,768]{1,0:T(8,128)(2,1)S(1)}, bf16[512,768]{1,0:T(8,128)(2,1)}, u32[]{:S(2)}) copy-start(bf16[512,768]{1,0:T(8,128)(2,1)} %copy-done.67) | copy-start | bytes 2359300
  166.1 86.5 %reduce-scatter.17.cloned.1.call-start = ((), (), s32[]{:S(2)}) async-start(), calls=%async_computation.17 | async-start | bytes 3145728 | tf_op jit(solution)/shard_map/reduce_scatter | solution.py:119
  228.9 34.5 %reduce-scatter.21.cloned.1.call-start = ((), (), s32[]{:S(2)}) async-start(), calls=%async_computation.20 | async-start | bytes 3145728 | tf_op jit(solution)/shard_map/reduce_scatter | solution.py:119
  246.0 6.4 copy-start.21
  246.0 6.4 copy-start.23
  252.5 29.1 %all-gather.19.cloned.1.call-start = ((), (), s32[]{:S(2)}) async-start(), calls=%async_computation.21 | async-start | bytes 3145728 | tf_op jit(solution)/shard_map/all_gather | solution.py:126
  269.7 26.0 %all-gather.17.cloned.1.call-start = ((), (), s32[]{:S(2)}) async-start(), calls=%async_computation.18 | async-start | bytes 3145728 | tf_op jit(solution)/shard_map/all_gather | solution.py:126
  270.3 38.7 %reduce-scatter.23.cloned.1.call-start = ((), (), s32[]{:S(2)}) async-start(), calls=%async_computation.22 | async-start | bytes 3145728 | tf_op jit(solution)/shard_map/reduce_scatter | solution.py:131
  281.6 10.1 %copy-start.89 = (bf16[1024,512]{1,0:T(8,128)(2,1)S(1)}, bf16[1024,512]{1,0:T(8,128)(2,1)}, u32[]{:S(2)}) copy-start(bf16[1024,512]{1,0:T(8,128)(2,1)} %param.37) | copy-start | bytes 3145732
  295.4 27.2 %reduce-scatter.19.cloned.1.call-start = ((), (), s32[]{:S(2)}) async-start(), calls=%async_computation.19 | async-start | bytes 3145728 | tf_op jit(solution)/shard_map/reduce_scatter | solution.py:131
  303.3 42.1 %all-gather.21.cloned.1.call-start = ((), (), s32[]{:S(2)}) async-start(), calls=%async_computation.23 | async-start | bytes 3145728 | tf_op jit(solution)/shard_map/all_gather | solution.py:176
  333.5 39.6 %reduce-scatter.25.cloned.1.call-start = ((), (), s32[]{:S(2)}) async-start(), calls=%async_computation.24 | async-start | bytes 3145728 | tf_op jit(solution)/shard_map/reduce_scatter | solution.py:185
  362.2 30.1 %all-gather.23.cloned.1.call-start = ((), (), s32[]{:S(2)}) async-start(), calls=%async_computation.25 | async-start | bytes 3145728 | tf_op jit(solution)/shard_map/all_gather | solution.py:196
  380.4 78.7 %reduce-scatter.27.cloned.1.call-start = ((), (), s32[]{:S(2)}) async-start(), calls=%async_computation.26 | async-start | bytes 3145728 | tf_op jit(solution)/shard_map/reduce_scatter | solution.py:207
  448.2 31.2 %all-gather.27.cloned.1.call-start = ((), (), s32[]{:S(2)}) async-start(), calls=%async_computation.30 | async-start | bytes 3145728 | tf_op jit(solution)/shard_map/all_gather | solution.py:176
  466.2 13.2 %copy-start.90 = (bf16[1024,512]{1,0:T(8,128)(2,1)S(1)}, bf16[1024,512]{1,0:T(8,128)(2,1)}, u32[]{:S(2)}) copy-start(bf16[1024,512]{1,0:T(8,128)(2,1)} %param.37) | copy-start | bytes 3145732
  467.5 39.2 %reduce-scatter.33.cloned.1.call-start = ((), (), s32[]{:S(2)}) async-start(), calls=%async_computation.31 | async-start | bytes 3145728 | tf_op jit(solution)/shard_map/reduce_scatter | solution.py:185
  492.0 14.7 %copy-start.63 = (f32[1024]{0:T(1024)S(1)}, f32[1024]{0:T(1024)}, u32[]{:S(2)}) copy-start(f32[1024]{0:T(1024)} %copy-done.62) | copy-start | bytes 12292
  492.0 14.7 %copy-start.66 = (f32[1024]{0:T(1024)S(1)}, f32[1024]{0:T(1024)}, u32[]{:S(2)}) copy-start(f32[1024]{0:T(1024)} %copy-done.65) | copy-start | bytes 12292
  495.8 11.0 %copy-start.2 = (bf16[1024,512]{1,0:T(8,128)(2,1)S(1)}, bf16[1024,512]{1,0:T(8,128)(2,1)}, u32[]{:S(2)}) copy-start(bf16[1024,512]{1,0:T(8,128)(2,1)} %param.27) | copy-start | bytes 3145732
  495.8 11.0 %copy-start.4 = (bf16[1024,512]{1,0:T(8,128)(2,1)S(1)}, bf16[1024,512]{1,0:T(8,128)(2,1)}, u32[]{:S(2)}) copy-start(bf16[1024,512]{1,0:T(8,128)(2,1)} %reduce-scatter.29.cloned.1.call-done) | copy-start | bytes 3145732
  495.8 13.9 %copy-start.73 = (f32[1024]{0:T(1024)S(1)}, f32[1024]{0:T(1024)}, u32[]{:S(2)}) copy-start(f32[1024]{0:T(1024)} %copy-done.72) | copy-start | bytes 12292
  495.8 29.8 %all-gather.29.cloned.1.call-start = ((), (), s32[]{:S(2)}) async-start(), calls=%async_computation.32 | async-start | bytes 3145728 | tf_op jit(solution)/shard_map/all_gather | solution.py:196
  513.7 179.1 %reduce-scatter.35.cloned.1.call-start = ((), (), s32[]{:S(2)}) async-start(), calls=%async_computation.33 | async-start | bytes 3145728 | tf_op jit(solution)/shard_map/reduce_scatter | solution.py:207
  583.0 5.7 copy-start.34
  583.0 244.0 %all-reduce.4.cloned.1.call-start = ((), (), s32[]{:S(2)}) async-start(), calls=%async_computation.34 | async-start | bytes 12582912 | tf_op jit(solution)/shard_map/psum | solution.py:230
  583.3 6.1 copy-start.86
  590.9 6.9 slice-start
  609.8 45.3 %copy-start.78 = (f32[512]{0:T(512)S(1)}, f32[512]{0:T(512)}, u32[]{:S(2)}) copy-start(f32[512]{0:T(512)} %get-tuple-element.376) | copy-start | bytes 6148
  609.8 45.3 %copy-start.77 = (f32[512]{0:T(512)S(1)}, f32[512]{0:T(512)}, u32[]{:S(2)}) copy-start(f32[512]{0:T(512)} %get-tuple-element.370) | copy-start | bytes 6148
  609.8 83.0 %copy-start.17 = (f32[1024,512]{1,0:T(8,128)S(1)}, f32[1024,512]{1,0:T(8,128)}, u32[]{:S(2)}) copy-start(f32[1024,512]{1,0:T(8,128)} %copy-done.16) | copy-start | bytes 6291460
  827.0 5.5 copy-start.53
  (76 other events, 186.6 us)
Sparse Core Ops, SparseCore 0:
  9.6 13.2 all-gather.10
  60.9 10.7 reduce-scatter.28
  89.3 10.7 reduce-scatter.12
  106.0 11.7 all-gather.24
  119.8 11.7 all-gather.12
  134.3 10.7 reduce-scatter.30
  148.0 10.8 reduce-scatter.14
  166.2 11.7 all-gather.14
  229.0 10.7 reduce-scatter.16
  252.6 10.7 reduce-scatter.20
  269.8 11.7 all-gather.18
  283.6 11.7 all-gather.16
  298.2 10.7 reduce-scatter.22
  311.8 10.8 reduce-scatter.18
  333.6 11.7 all-gather.20
  362.3 10.7 reduce-scatter.24
  380.5 11.7 all-gather.22
  448.3 10.7 reduce-scatter.26
  467.6 11.7 all-gather.26
  495.9 10.7 reduce-scatter.32
  513.8 11.7 all-gather.28
  583.1 10.7 reduce-scatter.34
  610.0 216.9 all-reduce.3
where the time goes:
time: 854 us; the launch traced here: 843 us
  waiting for transfers between devices  312 us (37%)
  matrix products  206 us (24%)
  local copies, waits for them, and re-layouts  162 us (19%)
  blocking collectives  82.3 us (10%)
  other arithmetic  61 us (7%)
  between operations  15.4 us (2%)
    psum x1, waiting for transfers between devices, reduce_grads(): wide = lax.psum(wide, 'dp')  131 us
    unnamed x198, local copies, waits for them, and re-layouts  46.1 us
    psum x1, blocking collectives, reduce_grads(): wide = lax.psum(wide, 'dp')  44.6 us
    reduce_scatter x4, waiting for transfers between devices, layer_forward(): lax.psum_scatter(jnp.dot(active, w_out, preferred_element_type=jnp.float3...  38.9 us
    psum x1, blocking collectives, reduce_grads(): small = lax.psum(small, ('dp', 'tensor'))  37.7 us
    dynamic_update_slice x32, local copies, waits for them, and re-layouts, attention(): lax.map(attend_block, pieces + (sent_lens.reshape(row_count // pair_size,...  31.9 us
    dot_general x16, matrix products, attend_block(): jnp.einsum('bhqk,bkhd->bqhd', probability, values, preferred_element_type...  29.7 us
    all_gather x4, waiting for transfers between devices, layer_forward(): lax.all_gather(middle.astype(jnp.bfloat16), 'tensor', axis=0, tiled=True)  24.5 us
  transfers between devices with their start and end apart: 23, of which 19 were waited for; matrix products, arithmetic and copies ran while one was open for 14% of the time, Pallas kernels for 0%

commit v1 on v0

v1 whole, which is shorter than its diff:
```python
import functools

import jax
import jax.numpy as jnp
from jax import lax
from jax.experimental import pallas as pl
from jax.experimental.pallas import tpu as pltpu
from jax.sharding import PartitionSpec as P

HEAD_DIM = 64
SEQ = 256
PAIR = 2 * HEAD_DIM
CHUNK = 512
BLOCK = 256
LEAST = 16
GROUP = 2
FORWARD_TURNS = (12, 1, 3, 1, 1, 8, 1, 1, 1, 3, 1, 1, 1, 2, 1, 1, 1, 1, 1, 2, 1, 3)
BACKWARD_TURNS = (8, 1, 1, 1, 1, 1, 1, 1, 1, 1, 1, 1, 1, 1, 1, 1)
LAST_TURNS = (3, 1, 1, 1, 1, 1, 1, 1, 1, 1, 1, 3)
ROWS = 32
EPS = 1e-05
MASKED = -1e30
SCALE = HEAD_DIM ** (-0.5)
GELU_A = 0.7978845608028654
GELU_B = GELU_A * 0.044715
BF16 = jnp.bfloat16
F32 = jnp.float32
MIB = 1 << 20
STEPS_AT = (
    (),
    (),
    ((0, 1),),
    ((1, 1),),
    ((0, 2), (2, 1)),
    ((1, 2),),
    ((0, 3),),
    ((1, 3), (3, 1)),
    (),
    ((4, 1),),
    ((3, 2),),
    ((2, 2), (5, 1)),
    ((0, 4),),
    ((1, 4), (4, 2)),
    ((3, 3), (0, 5)),
    ((2, 3),),
    ((1, 5),),
    ((3, 4), (5, 2)),
    ((4, 3),),
    ((0, 6), (3, 5)),
    ((2, 4), (6, 1), (1, 6)),
    ((4, 4), (5, 3), (7, 1), (8, 1)),
    ((2, 5), (0, 7), (3, 6)),
)
STEPS_LEFT = (
    (6, 2), (1, 7), (4, 5), (5, 4), (7, 2), (8, 2), (2, 6), (3, 7),
    (6, 3), (4, 6), (5, 5), (7, 3), (8, 3), (6, 4), (2, 7), (7, 4),
    (8, 4), (4, 7), (5, 6), (6, 5), (7, 5), (2, 8), (8, 5), (5, 7),
    (6, 6), (7, 6), (8, 6), (6, 7), (2, 9), (7, 7), (8, 7),
)
SMALL_AT = (7, 9, 12, 15, 18)
Z_FIRST = (2,)


def mm(a, b):
    return lax.dot_general(a, b, (((1,), (0,)), ((), ())), preferred_element_type=F32)


def mm_rt(a, b):
    return lax.dot_general(a, b, (((1,), (1,)), ((), ())), preferred_element_type=F32)


def mm_lt(a, b):
    return lax.dot_general(a, b, (((0,), (0,)), ((), ())), preferred_element_type=F32)


def low(v):
    return v.astype(BF16)


def norm(v):
    centred = v - jnp.mean(v, axis=-1, keepdims=True)
    root = lax.rsqrt(jnp.mean(centred * centred, axis=-1, keepdims=True) + EPS)
    return centred * root, root


def norm_back(d, n, root, gain):
    dn = d * gain
    first = jnp.mean(dn, axis=-1, keepdims=True)
    second = jnp.mean(dn * n, axis=-1, keepdims=True)
    return (dn - first - n * second) * root


def fold(v):
    return jnp.sum(v.reshape(v.shape[0] // 8, 8, v.shape[1]), axis=0)


def halves_by_rows(out, fn, n_sums, *arrays):
    joined, sums = [], None
    rows = arrays[0].shape[0]
    for r in range(0, rows, ROWS):
        got = fn(*(a[r : r + ROWS] for a in arrays))
        cut = len(got) - n_sums
        joined.append(got[:cut])
        sums = got[cut:] if sums is None else [a + b for a, b in zip(sums, got[cut:])]
        if r + ROWS == rows // 2:
            yield
    out += [jnp.concatenate(parts, axis=0) for parts in zip(*joined)]
    out += [jnp.sum(s, axis=0, keepdims=True) for s in sums]


def by_rows(fn, n_sums, *arrays):
    out = []
    for _ in halves_by_rows(out, fn, n_sums, *arrays):
        pass
    return out


def head_masks(dtype, value):
    lane = lax.broadcasted_iota(jnp.int32, (1, PAIR), 1)
    first = jnp.where(lane < HEAD_DIM, value, 0.0).astype(dtype)
    second = jnp.where(lane < HEAD_DIM, 0.0, value).astype(dtype)
    return first, second


def lanes(start, size):
    return pl.ds(pl.multiple_of(start, PAIR), size)


def interleave(first, second, turns):
    for i, turn in enumerate(turns):
        for _ in range(turn):
            next((first, second)[i % 2], None)
    for stream in (first, second):
        for _ in stream:
            pass


def attend(qkv, rows, probs, slab, d, key_bias, contexts):
    masks = head_masks(BF16, SCALE)
    heads = d // HEAD_DIM
    qs, ks, v_ts = [], [], []
    for col in range(0, d, PAIR):
        qs.append(qkv[rows, col : col + PAIR])
        ks.append(qkv[rows, d + col : d + col + PAIR])
        v_ts.append(qkv[rows, 2 * d + col : 2 * d + col + PAIR].T)
    scores, ps, halves = {}, {}, []
    for n in range(heads + 2):
        if n < heads:
            scores[n] = mm_rt(ks[n // 2], qs[n // 2] * masks[n % 2])
        if 1 <= n <= heads:
            full = scores.pop(n - 1)
            sides = []
            for c in range(0, SEQ, PAIR):
                s = full[:, c : c + PAIR] + key_bias
                e = jnp.exp(s - jnp.max(s, axis=0, keepdims=True))
                sides.append(low(e * (1.0 / jnp.sum(e, axis=0, keepdims=True))))
            ps[n - 1] = jnp.concatenate(sides, axis=1)
            probs[slab + n - 1] = ps[n - 1]
        if n >= 2:
            h = (n - 2) % 2
            halves.append(
                mm(v_ts[(n - 2) // 2][h * HEAD_DIM : (h + 1) * HEAD_DIM], ps.pop(n - 2))
            )
        yield
    contexts += [
        low(jnp.concatenate(halves[2 * i : 2 * i + 2], axis=0)) for i in range(heads // 2)
    ]


def attend_back(qkv, rows, probs, slab, d, grad_ctx, start, heads):
    masks, ones = head_masks(BF16, SCALE), head_masks(BF16, 1.0)
    qs, ks, vs, k_ts, gs = [], [], [], [], []
    for col in range(start * HEAD_DIM, (start + heads) * HEAD_DIM, PAIR):
        qs.append(qkv[rows, col : col + PAIR])
        ks.append(qkv[rows, d + col : d + col + PAIR])
        vs.append(qkv[rows, 2 * d + col : 2 * d + col + PAIR])
        k_ts.append(ks[-1].T)
        gs.append(grad_ctx[:, col - start * HEAD_DIM : col - start * HEAD_DIM + PAIR])
    d_p, g_hs, ps, d_s, d_q, out = {}, {}, {}, {}, {}, []
    for n in range(heads + 2):
        if n < heads:
            g_hs[n] = gs[n // 2] * ones[n % 2]
            ps[n] = probs[slab + start + n]
            d_p[n] = mm_rt(vs[n // 2], g_hs[n])
        if 1 <= n <= heads:
            full, p = d_p.pop(n - 1), ps[n - 1]
            sides = []
            for c in range(0, SEQ, PAIR):
                wide = p[:, c : c + PAIR].astype(F32)
                prod = full[:, c : c + PAIR] * wide
                sides.append(low(prod - wide * jnp.sum(prod, axis=0, keepdims=True)))
            d_s[n - 1] = jnp.concatenate(sides, axis=1)
        if n >= 2:
            m = n - 2
            pair, h = m // 2, m % 2
            d_q[m] = mm(k_ts[pair][h * HEAD_DIM : (h + 1) * HEAD_DIM], d_s[m])
            if h == 1:
                both = (m - 1, m)
                d_v = mm(
                    jnp.concatenate([ps[i] for i in both], axis=1),
                    jnp.concatenate([g_hs[i] for i in both], axis=0),
                )
                d_k = mm(
                    jnp.concatenate([d_s[i] for i in both], axis=1),
                    jnp.concatenate([qs[pair] * masks[i % 2] for i in both], axis=0),
                )
                q_t = low(jnp.concatenate([d_q[i] for i in both], axis=0) * SCALE)
                out.append((q_t.T, low(d_k), low(d_v)))
        yield
    for pair, grads in enumerate(out):
        for i, grad in enumerate(grads):
            col = i * d + start * HEAD_DIM + pair * PAIR
            qkv[rows, col : col + PAIR] = grad


def axis_sizes(n_dp):
    k = round((n_dp / 2) ** (1 / 3))
    return (k, k, 2 * k) if 2 * k**3 == n_dp else (1, 1, n_dp)


def unit_blocks(half_ff):
    n = half_ff // BLOCK
    tall_pairs = [(b, b + 1) for b in range(2, n, 2)]
    wide_pairs = [(b, b + 1) for b in range(n + 1, 2 * n + 1, 2)]
    return [(0,), (1,)] + tall_pairs + [(n,)] + wide_pairs + [(2 * n + i,) for i in range(1, 4)]


def unit_sizes(d, half_ff):
    return [d * len(blocks) for blocks in unit_blocks(half_ff)]


def unit_orders(count):
    return [(2, 3) if u in Z_FIRST else (0, 1) for u in range(count)]


def stage_plan(sizes, order, rows, coords):
    x, y, z = (((a, 1, sizes[a]),) for a in range(3))
    z_bits = tuple((2, 1 << b, 2) for b in range(sizes[2].bit_length() - 1))
    first, second = (y, x) if order % 2 else (x, y)
    walk = first + second + z if order < 2 else z_bits[:1] + first + second + z_bits[1:]
    off, plan = 0, []
    for axis, step, n in walk:
        if n == 1:
            continue
        at = coords[axis]
        place = (at // step) % n
        split = rows % (LEAST * n) == 0
        rows = rows // n if split else rows
        moves = []
        for k in range(1, n):
            to, back = (place + k) % n, (place + n - k) % n
            moves.append((
                at + (to - place) * step,
                off + to * rows if split else off,
                off + back * rows if split else off,
            ))
        off = off + place * rows if split else off
        plan.append((axis, split, rows, off, moves))
    return plan


def land_rows(sizes, units):
    orders = unit_orders(len(units))
    return sum(
        stage[2] * len(stage[4])
        for rows, halves in zip(units, orders)
        for order in halves
        for stage in stage_plan(sizes, order, rows // 2, (0, 0, 0))
    )


def layers_kernel(
    t_rows, sizes, lens, x_hbm, cot_hbm, wq_hbm, wk_hbm, wv_hbm, wo_hbm, w1_hbm, w2_hbm, b1_own,
    gain_a_ref, off_a_ref, bias_o_ref, gain_f_ref, off_f_ref,
    out_ref, gx_ref, gq_ref, gk_ref, gv_ref, go_ref, g1_ref, g2_ref, small_out,
    wqkv, w_o, w_1, w_2, b_1, b_half, x_buf, stream,
    qkv, probs, x_t, ctx_t, mid_t, act_n, gp, n_1, n_2, roots, g_ffn, g_attn,
    gb1_sum, theirs, whole, landing, small_v, small_r,
    in_sem, w_sem, w_send, w_recv, out_sem, put_sem, pair_send, pair_recv, send_sem, sum_recv,
    all_recv, done_sem, small_send, small_recv,
):
    d = w_o.shape[0]
    ff = w_1.shape[1]
    heads = d // HEAD_DIM
    group = x_buf.shape[0]
    per_group = group // SEQ
    n_groups = t_rows // group
    half_d, half_ff = d // 2, ff // 2
    side, dp = lax.axis_index("tensor"), lax.axis_index("dp")
    other = 1 - side
    gain_a, off_a, bias_o, gain_f, off_f = (
        r[...] for r in (gain_a_ref, off_a_ref, bias_o_ref, gain_f_ref, off_f_ref)
    )
    first = side * (t_rows // SEQ)
    strides = (1, sizes[0], sizes[0] * sizes[1])
    coords = tuple((dp // strides[a]) % sizes[a] for a in range(3))
    units = unit_sizes(d, half_ff)
    n_ffn = half_ff // BLOCK
    in_unit = unit_blocks(half_ff)
    n_blocks = 2 * n_ffn + 4
    unit_of = [u for u, blocks in enumerate(in_unit) for _ in blocks]
    tall = units[-1]

    def along(axis, to):
        return dp + (to - coords[axis]) * strides[axis]

    peers = [(dp, other)]
    for a in range(3):
        peers += [(along(a, (coords[a] + k) % sizes[a]), side) for k in range(1, sizes[a])]
    barrier = pltpu.get_barrier_semaphore()
    for peer in peers:
        pl.semaphore_signal(barrier, inc=1, device_id=peer, device_id_type=pl.DeviceIdType.MESH)
    pl.semaphore_wait(barrier, len(peers))

    def remote(src, dst, send, recv, dp_to, side_to):
        return pltpu.make_async_remote_copy(
            src_ref=src, dst_ref=dst, send_sem=send, recv_sem=recv,
            device_id=(dp_to, side_to), device_id_type=pl.DeviceIdType.MESH,
        )

    def span(i, n):
        return pl.ds(pl.multiple_of(i * n, n), n)

    def own_cols(base):
        return pl.ds(pl.multiple_of(base + side * half_d, half_d), half_d)

    weights = [
        (wq_hbm, wqkv.at[:, own_cols(0)]),
        (wk_hbm, wqkv.at[:, own_cols(d)]),
        (wv_hbm, wqkv.at[:, own_cols(2 * d)]),
        (wo_hbm, w_o.at[span(side, half_d), :]),
        (w1_hbm, w_1.at[:, span(side, half_ff)]),
        (w2_hbm, w_2.at[span(side, half_ff), :]),
    ]
    b_half[side] = b1_own[...].astype(F32)
    bias_copy = remote(
        b_half.at[side], b_half.at[side], w_send.at[6], w_recv.at[6], dp, other
    )
    for i, (src, dst) in enumerate(weights):
        if i == 5:
            bias_copy.start()
        remote(src, dst, w_send.at[i], w_recv.at[i], dp, other).start()
        pltpu.make_async_copy(src, dst, w_sem.at[i]).start()

    def have(now, indices):
        @pl.when(now == 0)
        def _():
            for i in indices:
                src, dst = weights[i]
                pltpu.make_async_copy(src, dst, w_sem.at[i]).wait()
                remote(src, dst, w_send.at[i], w_recv.at[i], dp, other).wait()
            if len(weights) - 1 in indices:
                bias_copy.wait()
                count, width = b_half.shape[1:]
                for n in range(2 * count):
                    b_1[:, n * width : (n + 1) * width] = b_half[n // count, n % count : n % count + 1, :]

    gb1_sum[...] = jnp.zeros_like(gb1_sum)
    small_v[0] = jnp.zeros_like(small_v[0])

    def at(layer, g):
        return pl.ds(pl.multiple_of(layer * t_rows + g * group, group), group)

    def at_sentence(layer, s):
        return pl.ds(pl.multiple_of(layer * t_rows + s * SEQ, SEQ), SEQ)

    def fetch_x(g):
        return pltpu.make_async_copy(x_hbm.at[at(0, g), :], x_buf, in_sem.at[0])

    def fetch_cot(g):
        return pltpu.make_async_copy(cot_hbm.at[at(0, g), :], x_buf, in_sem.at[1])

    fetch_x(0).start()

    kept = (t_rows // SEQ) * heads

    def slab_of(layer, s, in_group):
        return jnp.where(layer == 0, s, t_rows // SEQ + in_group) * heads

    n_chunks = ff // CHUNK

    def chunk(c):
        return slice(c * CHUNK, (c + 1) * CHUNK)

    def forward(g, layer, i):
        s = g * per_group + i
        rows, local = at_sentence(layer, s), slice(i * SEQ, (i + 1) * SEQ)
        x_low = low(stream[local, :])
        x_t[:, rows] = x_low.T
        for c in range(3 * d // CHUNK):
            qkv[rows, chunk(c)] = low(mm(x_low, wqkv[:, chunk(c)]))
            yield
        place = lax.broadcasted_iota(jnp.int32, (SEQ, PAIR), 0)
        key_bias = jnp.where(place < lens[first + s], 0.0, MASKED)
        contexts = []
        yield from attend(qkv, rows, probs, slab_of(layer, s, i), d, key_bias, contexts)
        for j, context in enumerate(contexts):
            ctx_t[j * PAIR : (j + 1) * PAIR, rows] = context
        context = jnp.concatenate([context.T for context in contexts], axis=1)
        if i == 0:
            have(g + layer, range(3, len(weights)))
        branch = mm(context, w_o[...])
        yield

        def first_norm(x, branch):
            n, root = norm(x + branch)
            middle = n * gain_a + off_a
            return low(n), root, middle + bias_o, low(middle)

        out = []
        yield from halves_by_rows(out, first_norm, 0, stream[local, :], branch)
        n, root, total, mid_low = out
        n_1[layer, local, :] = n
        roots[layer, local, 0:1] = root
        mid_t[:, rows] = mid_low.T
        yield
        hidden, acts = {}, {}
        for c in range(n_chunks + 2):
            if c < n_chunks:
                hidden[c] = mm(mid_low, w_1[:, chunk(c)])
            if 1 <= c <= n_chunks:
                last = chunk(c - 1)

                def activate(h):
                    h = low(h + b_1[:, last])
                    sq = h * h
                    t = jnp.tanh(h * (sq * GELU_B + GELU_A))
                    half_up = t * 0.5 + 0.5
                    act = h * half_up
                    return act, half_up + act * (1.0 - t) * (sq * (3.0 * GELU_B) + GELU_A)

                acts[c - 1], slope = by_rows(activate, 0, hidden.pop(c - 1))
                gp[rows, last] = slope
                act_n[rows, last] = acts[c - 1]
            if c >= 2:
                total = total + mm(acts.pop(c - 2), w_2[chunk(c - 2), :])
            yield

        def second_norm(v):
            n, root = norm(v)
            return low(n), root, n * gain_f + off_f

        out = []
        yield from halves_by_rows(out, second_norm, 0, total)
        n, root, result = out
        n_2[layer, local, :] = n
        roots[layer, local, 1:2] = root
        stream[local, :] = result
        yield

    def backward_norm(layer, g, i):
        rows, local = at_sentence(layer, g * per_group + i), slice(i * SEQ, (i + 1) * SEQ)

        def second_norm(grad, n, root):
            n = n.astype(F32)
            g_sum = norm_back(grad, n, root, gain_f)
            return g_sum, low(g_sum), fold(grad * n), fold(grad), fold(g_sum)

        out = []
        yield from halves_by_rows(
            out, second_norm, 3, stream[local, :], n_2[layer, local, :], roots[layer, local, 1:2]
        )
        g_mid, g_low, *sums = out
        for j, total in zip((2, 3, 4), sums):
            small_v[0, j : j + 1, :] += total
        g_ffn[rows, :] = g_low
        stream[local, :] = g_mid
        yield

    def backward_ffn(layer, g, i):
        rows, local = at_sentence(layer, g * per_group + i), slice(i * SEQ, (i + 1) * SEQ)
        g_mid, g_low = stream[local, :], g_ffn[rows, :]
        g_act, g_hid = {}, {}
        for c in range(n_chunks + 2):
            if c < n_chunks:
                g_act[c] = mm_rt(g_low, w_2[chunk(c), :])
            if 1 <= c <= n_chunks:
                last = chunk(c - 1)

                def through(g, slope):
                    g_h = g * slope.astype(F32)
                    return low(g_h), fold(g_h)

                g_hid[c - 1], total = by_rows(through, 1, g_act.pop(c - 1), gp[rows, last])
                gb1_sum[:, last] += total
                gp[rows, last] = g_hid[c - 1]
            if c >= 2:
                g_mid = g_mid + mm_rt(g_hid.pop(c - 2), w_1[:, chunk(c - 2)])
            yield

        def first_norm(grad, n, root):
            n = n.astype(F32)
            g_res = norm_back(grad, n, root, gain_a)
            return g_res, low(g_res), fold(grad * n), fold(grad)

        out = []
        yield from halves_by_rows(
            out, first_norm, 2, g_mid, n_1[layer, local, :], roots[layer, local, 0:1]
        )
        g_res, g_low, *sums = out
        for j, total in zip((0, 1), sums):
            small_v[0, j : j + 1, :] += total
        g_attn[rows, :] = g_low
        if layer == 1:
            stream[local, :] = g_res
        yield

    def backward_attn(layer, g, i, part, parts):
        s = g * per_group + i
        rows, some = at_sentence(layer, s), heads // parts
        at_part = slice(part * some * HEAD_DIM, (part + 1) * some * HEAD_DIM)
        grad_ctx = low(mm_rt(g_attn[rows, :], w_o[at_part, :]))
        yield
        yield from attend_back(
            qkv, rows, probs, slab_of(layer, s, i), d, grad_ctx, part * some, some
        )

    def backward(g, i):
        local = slice(i * SEQ, (i + 1) * SEQ)
        yield from backward_norm(1, g, i)
        yield from backward_ffn(1, g, i)
        yield from backward_attn(1, g, i, 0, 1)
        rows = at_sentence(1, g * per_group + i)
        total = stream[local, :]
        for c in range(3):
            at_third = slice(c * d, (c + 1) * d)
            total = total + mm_rt(qkv[rows, at_third], wqkv[:, at_third])
            if c == 2:
                stream[local, :] = total
            yield
        yield from backward_norm(0, g, i)

    def both(steps_of, turns):
        if per_group == 2:
            interleave(steps_of(0), steps_of(1), turns)
        else:
            for _ in steps_of(0):
                pass

    starts = [sum(units[:u]) for u in range(len(units))]
    plans, landed = [], 0
    for rows, orders in zip(units, unit_orders(len(units))):
        halves = []
        for order in orders:
            plan = []
            for axis, split, n, own, moves in stage_plan(sizes, order, rows // 2, coords):
                plan.append((axis, split, n, own, moves, landed))
                landed += n * len(moves)
            halves.append(plan)
        plans.append(halves)
    stages = [max(len(plan) for plan in halves) for halves in plans]

    def unit_rows(u, half, start, n):
        return pl.ds(pl.multiple_of(starts[u] + half * (units[u] // 2) + start, LEAST), n)

    def acc_at(start, n):
        return probs.at[kept + start // BLOCK, pl.ds(pl.multiple_of(start % BLOCK, LEAST), n), :]

    def half_row(u, half, start):
        return starts[u] + half * (units[u] // 2) + start

    def pair_copy(b):
        return remote(
            theirs.at[b % 2], whole.at[b * tall : (b + 1) * tall, :],
            pair_send.at[b], pair_recv.at[unit_of[b]], dp, other,
        )

    def send_sums(u, half, i):
        axis, _, n, _, moves, land = plans[u][half][i]
        for k, (to, give, _) in enumerate(moves):
            remote(
                acc_at(half_row(u, half, give), n), landing.at[land + k * n : land + (k + 1) * n, :],
                send_sem.at[u], sum_recv.at[u, half, i], along(axis, to), side,
            ).start()

    def send_all(u, half, i):
        while i >= 0 and not plans[u][half][i][1]:
            i -= 1
        if i < 0:
            return
        axis, _, n, own, moves, _ = plans[u][half][i]
        for to, _, _ in moves:
            rows = unit_rows(u, half, own, n)
            remote(
                whole.at[rows, :], whole.at[rows, :], send_sem.at[u], all_recv.at[u, half, i],
                along(axis, to), side,
            ).start()

    def arrived(rows, sem):
        pltpu.make_async_copy(whole.at[0:rows, :], whole.at[0:rows, :], sem).wait()

    def sent_rows(u):
        return sum(
            n * len(moves) * (2 if split else 1)
            for plan in plans[u]
            for _, split, n, _, moves, _ in plan
        )

    def done_copies(u):
        copies = []
        for b in in_unit[u]:
            if b > n_ffn:
                first_col = (b - n_ffn - 1) * BLOCK
                out = (
                    g1_ref.at[:, first_col : first_col + BLOCK] if b <= 2 * n_ffn
                    else (gq_ref, gk_ref, gv_ref)[b - 2 * n_ffn - 1]
                )
                copies.append(pltpu.make_async_copy(
                    whole.at[b * tall : (b + 1) * tall, :], out, done_sem.at[b, 0]
                ))
                continue
            for c in range(2):
                row = b * tall + c * BLOCK
                cols = slice(c * BLOCK, (c + 1) * BLOCK)
                rows = slice(b * BLOCK, (b + 1) * BLOCK)
                out = g2_ref.at[rows, cols] if b < n_ffn else go_ref.at[:, cols]
                copies.append(pltpu.make_async_copy(
                    whole.at[row : row + BLOCK, :], out, done_sem.at[b, c]
                ))
        return copies

    def step_pair(u):
        arrived(units[u], pair_recv.at[u])

        def add(i, carry):
            rows = pl.ds(pl.multiple_of(starts[u] + i * BLOCK, BLOCK), BLOCK)
            at_slab = kept + starts[u] // BLOCK + i
            probs[at_slab] = probs[at_slab] + whole[rows, :]
            return carry

        lax.fori_loop(0, units[u] // BLOCK, add, 0)
        for half in range(2):
            send_sums(u, half, 0)

    def step_sum(i, u):
        for half in range(2):
            if i >= len(plans[u][half]):
                continue
            _, _, n, own, moves, land = plans[u][half][i]
            arrived(n * len(moves), sum_recv.at[u, half, i])
            mine = acc_at(half_row(u, half, own), n)
            total = mine[...]
            for k in range(len(moves)):
                total = total + landing[land + k * n : land + (k + 1) * n, :]
            if i + 1 < len(plans[u][half]):
                mine[...] = total
                send_sums(u, half, i + 1)
            else:
                whole[unit_rows(u, half, own, n), :] = total
                send_all(u, half, i)

    def step_all(i, u):
        for half in range(2):
            if i < len(plans[u][half]) and plans[u][half][i][1]:
                _, _, n, _, moves, _ = plans[u][half][i]
                arrived(n * len(moves), all_recv.at[u, half, i])
                send_all(u, half, i - 1)
        if i == 0:
            for copy in done_copies(u):
                copy.start()

    def run_step(u, step):
        if step == 1:
            step_pair(u)
        elif step <= 1 + stages[u]:
            step_sum(step - 2, u)
        else:
            step_all(2 * stages[u] + 1 - step, u)

    small_peers = [(dp, other)]
    bits = (sizes[0] * sizes[1] * sizes[2]).bit_length() - 1
    for bit in range(bits):
        small_peers.append((dp + (1 << bit) * (1 - 2 * ((dp // (1 << bit)) % 2)), side))

    def small_copy(i):
        return remote(
            small_v.at[i], small_r.at[i], small_send.at[i], small_recv.at[i], *small_peers[i]
        )

    def run_small(i):
        small_copy(i).wait()
        small_v[i + 1] = small_v[i] + small_r[i]
        if i + 1 < len(small_peers):
            small_copy(i + 1).start()

    def plain_schedule():
        at_block = list(range(n_ffn)) + [n_ffn + 1 + i for i in range(n_ffn + 1)]
        at_block += [len(STEPS_AT) - 5 + i for i in range(3)]
        born = [at_block[blocks[-1]] for blocks in in_unit]
        count = max(born[u] + 2 * stages[u] + 1 for u in range(len(units))) + 1
        at = [
            [(u, now - born[u]) for u in range(len(units)) if 1 <= now - born[u] <= 2 * stages[u] + 1]
            for now in range(count)
        ]
        return at[: len(STEPS_AT)], [step for now in at[len(STEPS_AT) :] for step in now]

    usual = sizes == (2, 2, 4) and len(units) == 9
    steps_at, steps_left = (STEPS_AT, STEPS_LEFT) if usual else plain_schedule()

    def tick(now):
        if now in SMALL_AT and SMALL_AT.index(now) < len(small_peers):
            run_small(SMALL_AT.index(now))
        for u, step in steps_at[now]:
            run_step(u, step)

    def ticks(i, count, base, stride=1):
        for k in range(count):
            @pl.when(i == k)
            def _():
                tick(base + stride * k)

    def launch(b, value_of):
        def cut(value):
            if value.shape[1] == BLOCK:
                return low(value[:BLOCK]), low(value[BLOCK:])
            return low(value[:, :BLOCK]), low(value[:, BLOCK:])

        for_other, own = cut(value_of(other)), cut(value_of(side))

        @pl.when(b >= 2)
        def _():
            arrived(tall, pair_send.at[b - 2])

        for i in range(2):
            theirs[b % 2, i * BLOCK : (i + 1) * BLOCK, :] = for_other[i]
            probs[kept + 2 * b + i] = own[i]

    def go(i, count, first_block, first_tick):
        for k in range(count):
            @pl.when(i == k)
            def _():
                pair_copy(first_block + k).start()
                tick(first_tick + k)

    def hidden(j, which):
        return pl.ds(pl.multiple_of(which * half_ff + j * BLOCK, BLOCK), BLOCK)

    def out_blocks(j, carry):
        launch(j, lambda which: mm_lt(act_n[:, hidden(j, which)], g_ffn[...]))
        go(j, n_ffn, 0, 0)
        return carry

    def main(g, carry):
        rows = at(0, g)
        fetch_x(g).wait()
        stream[...] = x_buf[...].astype(F32)
        fetch_cot(g).start()
        have(g, range(3))

        def one_layer(layer, inner):
            both(functools.partial(forward, g, layer), FORWARD_TURNS)
            return inner

        lax.fori_loop(0, 2, one_layer, 0)

        put_out = []
        for i in range(group // BLOCK):
            for c in range(d // BLOCK):
                n = per_group * heads + i * (d // BLOCK) + c
                at_cols = slice(c * BLOCK, (c + 1) * BLOCK)
                probs[kept + n] = low(stream[i * BLOCK : (i + 1) * BLOCK, at_cols])
                put_out.append(pltpu.make_async_copy(
                    probs.at[kept + n], out_ref.at[pl.ds(g * group + i * BLOCK, BLOCK), at_cols],
                    put_sem.at[i, c],
                ))
                put_out[-1].start()
        fetch_cot(g).wait()
        stream[...] = x_buf[...].astype(F32)

        @pl.when(g + 1 < n_groups)
        def _():
            fetch_x(g + 1).start()


        both(functools.partial(backward, g), BACKWARD_TURNS)
        for copy in put_out:
            copy.wait()

        @pl.when(g == n_groups - 1)
        def _():
            lax.fori_loop(0, n_ffn, out_blocks, 0)

        both(functools.partial(backward_ffn, 0, g), LAST_TURNS)
        return carry

    lax.fori_loop(0, n_groups, main, 0)
    for c in range(ff // d):
        small_v[0, 8 + c : 9 + c, :] = gb1_sum[:, c * d : (c + 1) * d]

    small_copy(0).start()
    tick(n_ffn)

    launch(n_ffn, lambda which: mm(ctx_t[span(which, half_d), :], g_attn[...]))
    pair_copy(n_ffn).start()
    tick(n_ffn + 1)

    def in_blocks(j, carry):
        launch(n_ffn + 1 + j, lambda which: mm(mid_t[...], gp[:, hidden(j, which)]))
        go(j, n_ffn, n_ffn + 1, n_ffn + 2)
        return carry

    lax.fori_loop(0, n_ffn, in_blocks, 0)
    tick_back = 2 * n_ffn + 2
    tick_q = tick_back + n_groups * per_group * 2

    def back_1(s, carry):
        for part in range(2):
            for _ in backward_attn(0, s // per_group, s % per_group, part, 2):
                pass
            ticks(s, n_groups * per_group, tick_back + part, 2)
        return carry

    lax.fori_loop(0, n_groups * per_group, back_1, 0)

    def qkv_blocks(i, carry):
        launch(
            2 * n_ffn + 1 + i,
            lambda which: mm(x_t[...], qkv[:, lanes(i * d + which * half_d, half_d)]),
        )
        go(i, 3, 2 * n_ffn + 1, tick_q)
        return carry

    lax.fori_loop(0, 3, qkv_blocks, 0)

    def grad_x(g, carry):
        rows = at(0, g)

        @pl.when(g > 0)
        def _():
            pltpu.make_async_copy(x_buf, gx_ref.at[rows, :], out_sem).wait()

        x_buf[...] = low(g_attn[rows, :].astype(F32) + mm_rt(qkv[rows, :], wqkv[...]))
        pltpu.make_async_copy(x_buf, gx_ref.at[rows, :], out_sem).start()
        ticks(g, n_groups, tick_q + 3)
        return carry

    lax.fori_loop(0, n_groups, grad_x, 0)
    for now in range(tick_q + 3 + n_groups, len(steps_at)):
        tick(now)
    for u, step in steps_left:
        run_step(u, step)
    for i in range(len(small_peers)):
        if i >= len(SMALL_AT):
            run_small(i)
    for b in range(n_blocks - 2, n_blocks):
        arrived(tall, pair_send.at[b])
    for u in range(len(units)):
        arrived(sent_rows(u), send_sem.at[u])
    pltpu.make_async_copy(x_buf, gx_ref.at[at(0, 0), :], out_sem).wait()
    small_out[...] = small_v[len(small_peers)]
    for u in range(len(units)):
        for copy in done_copies(u):
            copy.wait()


def layers(n_dp, lens, x, cot, w_q, w_k, w_v, w_o, w_1, w_2, b_1, vectors):
    t_rows, d = x.shape
    half_ff = w_1.shape[1]
    ff = 2 * half_ff
    half_d = d // 2
    heads = d // HEAD_DIM
    sentences = t_rows // SEQ
    group = SEQ * (GROUP if sentences % GROUP == 0 else 1)
    sizes = axis_sizes(n_dp)
    units = unit_sizes(d, half_ff)
    most = 2 + sizes[2].bit_length()
    n_small = n_dp.bit_length()
    vmem = pl.BlockSpec(memory_space=pltpu.VMEM)
    hbm = pl.BlockSpec(memory_space=pl.ANY)
    dma = pltpu.SemaphoreType.DMA
    return pl.pallas_call(
        functools.partial(layers_kernel, t_rows, sizes),
        out_shape=(
            jax.ShapeDtypeStruct((t_rows, d), BF16),
            jax.ShapeDtypeStruct((t_rows, d), BF16),
            jax.ShapeDtypeStruct((d, half_d), BF16),
            jax.ShapeDtypeStruct((d, half_d), BF16),
            jax.ShapeDtypeStruct((d, half_d), BF16),
            jax.ShapeDtypeStruct((half_d, d), BF16),
            jax.ShapeDtypeStruct((d, half_ff), BF16),
            jax.ShapeDtypeStruct((half_ff, d), BF16),
            jax.ShapeDtypeStruct((16, d), F32),
        ),
        in_specs=[pl.BlockSpec(memory_space=pltpu.SMEM)] + [hbm] * 8 + [vmem] * 6,
        out_specs=(hbm,) * 8 + (vmem,),
        scratch_shapes=[
            pltpu.VMEM((d, 3 * d), BF16),
            pltpu.VMEM((d, d), BF16),
            pltpu.VMEM((d, ff), BF16),
            pltpu.VMEM((ff, d), BF16),
            pltpu.VMEM((1, ff), F32),
            pltpu.VMEM((2, 8, half_ff // 8), F32),
            pltpu.VMEM((group, d), BF16),
            pltpu.VMEM((group, d), F32),
            pltpu.VMEM((2 * t_rows, 3 * d), BF16),
            pltpu.VMEM((sentences * heads + max(2 * heads + group // BLOCK * d // BLOCK, sum(units) // BLOCK), SEQ, SEQ), BF16),
            pltpu.VMEM((d, 2 * t_rows), BF16),
            pltpu.VMEM((d, 2 * t_rows), BF16),
            pltpu.VMEM((d, 2 * t_rows), BF16),
            pltpu.VMEM((2 * t_rows, ff), BF16),
            pltpu.VMEM((2 * t_rows, ff), BF16),
            pltpu.VMEM((2, group, d), BF16),
            pltpu.VMEM((2, group, d), BF16),
            pltpu.VMEM((2, group, 2), F32),
            pltpu.VMEM((2 * t_rows, d), BF16),
            pltpu.VMEM((2 * t_rows, d), BF16),
            pltpu.VMEM((1, ff), F32),
            pltpu.VMEM((2, d, BLOCK), BF16),
            pltpu.VMEM((sum(units), BLOCK), BF16),
            pltpu.VMEM((land_rows(sizes, units), BLOCK), BF16),
            pltpu.VMEM((n_small + 1, 16, d), F32),
            pltpu.VMEM((n_small, 16, d), F32),
            dma((2,)),
            dma((7,)),
            dma((7,)),
            dma((7,)),
            dma,
            dma((group // BLOCK, d // BLOCK)),
            dma((sum(units) // d,)),
            dma((len(units),)),
            dma((len(units),)),
            dma((len(units), 2, most)),
            dma((len(units), 2, most)),
            dma((sum(units) // d, 2)),
            dma((n_small,)),
            dma((n_small,)),
        ],
        compiler_params=pltpu.CompilerParams(
            vmem_limit_bytes=63 * MIB, collective_id=0, has_side_effects=True
        ),
        name="layers",
    )(lens, x, cot, w_q, w_k, w_v, w_o, w_1, w_2, b_1, *vectors)


def widen_kernel(per_side, small, *refs):
    count = (len(refs) - 6) // 2
    for src, dst in zip(refs[:count], refs[count : 2 * count]):
        dst[...] = src[...].astype(dst.dtype)
    side = lax.axis_index("tensor")
    for i, ref in enumerate(refs[2 * count : -1]):
        ref[...] = small[i : i + 1, :]
    d = small.shape[1]
    for c in range(per_side):
        first, second = (small[8 + s * per_side + c : 9 + s * per_side + c, :] for s in range(2))
        refs[-1][:, c * d : (c + 1) * d] = jnp.where(side == 0, first, second)


def widen(small, out, wide, half_ff):
    steps = 2
    d = small.shape[1]
    arrays = [out] + wide
    rows = [jax.ShapeDtypeStruct((1, d), F32)] * 5 + [jax.ShapeDtypeStruct((1, half_ff), F32)]

    def cut(a):
        return pl.BlockSpec((a.shape[0] // steps, a.shape[1]), lambda i: (i, 0))

    def fixed(a):
        return pl.BlockSpec(a.shape, lambda i: (0, 0))

    return pl.pallas_call(
        functools.partial(widen_kernel, half_ff // d),
        grid=(steps,),
        out_shape=[jax.ShapeDtypeStruct(out.shape, BF16)]
        + [jax.ShapeDtypeStruct(a.shape, F32) for a in wide]
        + rows,
        in_specs=[fixed(small)] + [cut(a) for a in arrays],
        out_specs=[cut(a) for a in arrays] + [fixed(r) for r in rows],
        compiler_params=pltpu.CompilerParams(vmem_limit_bytes=62 * MIB),
        name="widen",
    )(small, *arrays)


def shards(
    n_dp, inputs, lengths, w_query, w_key, w_value, w_attn_out, gain_attn, offset_attn,
    w_in, b_in, w_out, b_out, gain_ffn, offset_ffn, cotangent,
):
    vectors = [v[None] for v in (gain_attn, offset_attn, b_out, gain_ffn, offset_ffn)]
    out, *wide, small = layers(
        n_dp, lengths, inputs, cotangent, w_query, w_key, w_value, w_attn_out, w_in, w_out,
        b_in.reshape(8, -1), vectors,
    )
    out, gx, g_q, g_k, g_v, g_o, g_1, g_2, s0, s1, s2, s3, s4, gb1 = widen(
        small, out, wide, b_in.shape[0]
    )
    return (
        out, gx, g_q, g_k, g_v, g_o, s0[0], s1[0], g_1, gb1[0], g_2, s4[0], s2[0], s3[0],
    )


def solution(mesh):
    rows = P(("dp", "tensor"), None)
    cols, tall, whole = P(None, "tensor"), P("tensor", None), P()
    in_specs = (
        rows, P("dp"), cols, cols, cols, tall, whole, whole,
        cols, P("tensor"), tall, whole, whole, whole, rows,
    )
    out_specs = (
        rows, rows, cols, cols, cols, tall, whole, whole,
        cols, P("tensor"), tall, whole, whole, whole,
    )
    return jax.shard_map(
        functools.partial(shards, mesh.shape["dp"]), mesh=mesh, in_specs=in_specs, out_specs=out_specs,
        check_vma=False,
    )
```

time: 854 us -> 130 us (0.15); the launches traced: 843 us -> 130 us
  waiting for transfers between devices: 312 us -> 0 us
  matrix products: 206 us -> 0 us
  local copies, waits for them, and re-layouts: 162 us -> 0 us
  Pallas kernels: 0 us -> 129 us
  blocking collectives: 82.3 us -> 0 us
  other arithmetic: 61 us -> 0 us
  between operations: 15.4 us -> 0.82 us
    dot_general x92 -> x0, matrix products: 185 us -> none  [the longest x16 29.7 us: attend_block(): jnp.einsum('bhqk,bkhd->bqhd', probability, values, preferred_element_type...]
    psum x1 -> x0, waiting for transfers between devices: 131 us -> none  [reduce_grads(): wide = lax.psum(wide, 'dp')]
    pallas_call x0 -> x2, Pallas kernels: none -> 129 us  [the longest x1 123 us: layers(): pl.pallas_call(functools.partial(layers_kernel, t_rows, sizes), out_shape...]
    reduce_scatter x12 -> x0, waiting for transfers between devices: 90 us -> none  [the longest x4 38.9 us: layer_forward(): lax.psum_scatter(jnp.dot(active, w_out, preferred_element_type=jnp.float3...]
    all_gather x10 -> x0, waiting for transfers between devices: 89.1 us -> none  [the longest x4 24.5 us: layer_forward(): lax.all_gather(middle.astype(jnp.bfloat16), 'tensor', axis=0, tiled=True)]
    psum x2 -> x0, blocking collectives: 82.3 us -> none  [the longest x1 44.6 us: reduce_grads(): wide = lax.psum(wide, 'dp')]
    unnamed x198 -> x0, local copies, waits for them, and re-layouts: 46.1 us -> none
    reshape x19 -> x0, local copies, waits for them, and re-layouts: 43.7 us -> none  [the longest x8 21.4 us: to_blocks(): matrix.reshape(row_count // pair_size, pair_size, SEQ, head_count, HEAD_DIM)]
  transfers between devices with their start and end apart: 23 -> 0, of which waited for: 19 -> 0; matrix products, arithmetic and copies ran while one was open for 14% -> 0% of each run, Pallas kernels for 0% -> 0%
where the time goes in v1:
time: 130 us
  Pallas kernels  129 us (99%)
    pallas_call x1, Pallas kernels, layers(): pl.pallas_call(functools.partial(layers_kernel, t_rows, sizes), out_shape...  123 us
    pallas_call x1, Pallas kernels, widen(): pl.pallas_call(functools.partial(widen_kernel, half_ff // d), grid=(steps...  5.89 us

profile of v1, /device:TPU:0, one launch (start us, length us, event | category | flops | bytes accessed | tf_op | source)
XLA Modules:
  0.0 129.8 jit_solution(16301504981458962662)
XLA Ops:
  0.7 123.1 %layers.1 = (bf16[1024,512]{1,0:T(8,128)(2,1)}, bf16[1024,512]{1,0:T(8,128)(2,1)}, bf16[512,256]{1,0:T(8,128)(2,1)}, bf16[512,256]{1,0:T(8,128)(2,1)}, bf16[512,...) custom-call(s32[8]{0:T(128)} %lens.1, ...), custom_call_target="tpu_custom_call" | custom-call | tf_op jit(solution)/shard_map/layers/pallas_call | solution.py:871
  123.7 5.9 %widen.1 = (bf16[1024,512]{1,0:T(8,128)(2,1)}, f32[1024,512]{1,0:T(8,128)}, f32[512,256]{1,0:T(8,128)}, f32[512,256]{1,0:T(8,128)}, f32[512,256]{1,0:T(8,128)}, ...) custom-call(f32[16,512]{1,0:T(8,128)} %get-tuple-element.37.small, ...), custom_call_target="tpu_custom_call" | custom-call | tf_op jit(solution)/shard_map/widen/pallas_call | solution.py:960
